TPU v7x, 32 devices: a whole 2x2x4 slice. The times are simulated.
32 devices in a mesh: groups: 2 (over x), fsdp: 16 (over z, y, core).
Axes of the slice: x: 2, y: 2, z: 4, core: 2. Of those that a mesh axis runs over, the one named last changes fastest.
Arguments:
- acts: bfloat16 [8192, 8192], P(('groups', 'fsdp')), parts along dimension 0, may hold values from -6 to 6
- cotangent: bfloat16 [4096, 1024], P(('groups', 'fsdp')), parts along dimension 0, may hold values from -6 to 6
- plan: int32 [64], P('groups'), parts along dimension 0, may hold values from -1 to 15, as said below
- source_block_length: int32 [64], P('groups'), parts along dimension 0, may hold values from 0 to 128, as said below
- source_block_job: int32 [64], P('groups'), parts along dimension 0, may hold values from 0 to 7
- frozen_value_weight: bfloat16 [8192, 1024], P('fsdp'), may hold values from -0.0625 to 0.0625
- adapter_down_weight: bfloat16 [16384, 128], P(('groups', 'fsdp')), parts along dimension 0, may hold values from -0.0625 to 0.0625
- adapter_up_weight: bfloat16 [256, 1024], P('groups'), parts along dimension 0, may hold values from -0.1875 to 0.1875
Outputs:
- values: bfloat16 [4096, 1024], P(('groups', 'fsdp')), parts along dimension 0
- layer_input_gradient: bfloat16 [8192, 8192], P(('groups', 'fsdp')), parts along dimension 0
- down_grad: float32 [16384, 128], P(('groups', 'fsdp')), parts along dimension 0
- up_weight_gradient: float32 [256, 1024], P('groups'), parts along dimension 0
There are 2 independent parts, one for each index of `groups`. A program takes and returns all parts, laid end to end along the dimension named above; an argument that names none is the same for every part. Nothing has to cross between parts.
Inputs may be any that keep to these rules, and one draw needn't show every extreme that they name: Device i holds source slots i * 2 to i * 2 + 1. plan is -1 exactly where source_block_length is 0; otherwise it is i or i + 1, and no two slots share a value, so each balanced block receives at most one slot. Which slot of a device holds which block varies. `source_block_length`: live tokens are the first ones of a block; some block is full in every draw.
All inputs are finite; a program needn't handle non-finite values.
Results may differ from a plain program's by a relative error of at most 0.0031.
Values may be sent and summed in bfloat16 or wider, within the bound.
A program may use at most 128 MiB of HBM per device.

v0:
```python
import jax
import jax.numpy as jnp
from jax import lax
from jax.sharding import PartitionSpec as P

ADAPTER_RANK = 16
BLK = 128


ADAPTER_SCALE = 2.0


def shifted(value, axis, by):
    length = lax.axis_size(axis)
    pairs = [(i, i + by) for i in range(length) if 0 <= i + by < length]
    return lax.ppermute(value, axis, pairs)


def contract_trailing(left, right):
    return lax.dot_general(
        left, right, (((1,), (1,)), ((), ())), preferred_element_type=jnp.float32
    )


def contract_leading(left, right):
    return lax.dot_general(
        left, right, (((0,), (0,)), ((), ())), preferred_element_type=jnp.float32
    )


def pick_block(stacked, slot_number):
    return lax.dynamic_index_in_dim(stacked, slot_number, 0, keepdims=False)


def adapted_output(
    input_rows,
    masked_output_gradient,
    job_column_span,
    live_token_mask,
    frozen_value_weight,
    adapter_down_weight,
    adapter_up_weight,
):
    hidden_state = (
        ADAPTER_SCALE
        * contract_trailing(masked_output_gradient, adapter_up_weight)
        * job_column_span
    ).astype(jnp.bfloat16)
    down_weight_whole = lax.all_gather(adapter_down_weight, "fsdp", axis=0, tiled=True)
    reduced = jnp.dot(input_rows, down_weight_whole, preferred_element_type=jnp.float32)
    piece = lax.all_gather(frozen_value_weight, "fsdp", axis=0, tiled=True)
    projected_value = jnp.dot(input_rows, piece, preferred_element_type=jnp.float32)
    grad_piece = contract_trailing(masked_output_gradient, piece) + contract_trailing(
        hidden_state, down_weight_whole
    )
    grads = grad_piece
    projected_value, grads = (projected_value, grads)
    reduced_rank_state = (reduced * job_column_span).astype(jnp.bfloat16)
    output_rows = projected_value + ADAPTER_SCALE * jnp.dot(
        reduced_rank_state, adapter_up_weight, preferred_element_type=jnp.float32
    )
    output_rows = (output_rows * live_token_mask[:, None]).astype(jnp.bfloat16)
    return (output_rows, grads.astype(jnp.bfloat16), reduced_rank_state, hidden_state)


def body(
    acts,
    cotangent,
    plan,
    source_block_length,
    source_block_job,
    frozen_value_weight,
    adapter_down_weight,
    adapter_up_weight,
):
    device_index = lax.axis_index("fsdp")
    slot_count = acts.shape[0] // BLK
    feature_width = acts.shape[1]
    column_span = jnp.arange(adapter_down_weight.shape[1], dtype=jnp.int32) // ADAPTER_RANK
    positions = jnp.arange(BLK, dtype=jnp.int32)
    local_plan = lax.dynamic_slice_in_dim(plan, device_index * slot_count, slot_count)
    own_flags = local_plan == device_index
    right_flags = local_plan == device_index + 1
    own_slot = jnp.argmax(own_flags)
    has_own = jnp.any(own_flags)
    right_slot = jnp.argmax(right_flags)
    has_right = jnp.any(right_flags)
    arrivals = plan == device_index
    has_arrival = jnp.any(arrivals)
    anchor = jnp.argmax(arrivals)
    from_left = has_arrival & (anchor // slot_count != device_index)
    blocks = acts.reshape(slot_count, BLK, feature_width)
    outgoing = jnp.where(
        has_right, pick_block(blocks, right_slot), jnp.zeros((BLK, feature_width), acts.dtype)
    )
    incoming = shifted(outgoing, "fsdp", 1)
    input_rows = jnp.where(from_left, incoming, pick_block(blocks, own_slot))
    dest_len = jnp.where(has_arrival, source_block_length[anchor], 0)
    dest_job = source_block_job[anchor]
    live_token_mask = (positions < dest_len).astype(jnp.float32)
    masked_output_gradient = jnp.where(
        live_token_mask[:, None] > 0, cotangent, jnp.zeros_like(cotangent)
    )
    job_column_span = (column_span[None, :] == dest_job).astype(jnp.float32)
    values, grads, reduced_rank_state, hidden_state = adapted_output(
        input_rows,
        masked_output_gradient,
        job_column_span,
        live_token_mask,
        frozen_value_weight,
        adapter_down_weight,
        adapter_up_weight,
    )
    zero_grad = jnp.zeros_like(grads)
    returned = shifted(jnp.where(from_left, grads, zero_grad), "fsdp", -1)
    own_grad = jnp.where(has_arrival & jnp.logical_not(from_left), grads, zero_grad)
    grad_slots = []
    for slot_number in range(slot_count):
        grad_slots.append(
            jnp.where(
                has_own & (own_slot == slot_number),
                own_grad,
                jnp.where(has_right & (right_slot == slot_number), returned, zero_grad),
            )
        )
    layer_input_gradient = jnp.stack(grad_slots, 0).reshape(slot_count * BLK, feature_width)
    owned_columns = lax.all_to_all(input_rows, "fsdp", split_axis=1, concat_axis=0, tiled=True)
    every_hidden = lax.all_gather(hidden_state, "fsdp", axis=0, tiled=True)
    down_grad = contract_leading(owned_columns, every_hidden)
    up_weight_gradient = lax.psum(
        ADAPTER_SCALE * contract_leading(reduced_rank_state, masked_output_gradient), "fsdp"
    )
    return (values, layer_input_gradient, down_grad, up_weight_gradient)


def solution(mesh):
    placed = (
        P(("groups", "fsdp"), None),
        P(("groups", "fsdp"), None),
        P("groups"),
        P("groups"),
        P("groups"),
        P("fsdp", None),
        P(("groups", "fsdp"), None),
        P("groups", None),
    )
    return jax.shard_map(
        body,
        mesh=mesh,
        in_specs=placed,
        out_specs=(
            P(("groups", "fsdp"), None),
            P(("groups", "fsdp"), None),
            P(("groups", "fsdp"), None),
            P("groups", None),
        ),
        check_vma=False,
    )
```

profile of v0, /device:TPU:8, one launch (start us, length us, event | category | flops | bytes accessed | tf_op | source)
XLA Modules:
  0.0 350.2 jit_solution(10636967129604953564)
XLA Ops:
  7.2 0.7 all-gather.3.cloned.1.call-update
  8.0 1.4 compare_reduce_fusion
  11.9 2.4 select_bitcast_fusion.2
  14.3 1.9 collective-permute-start
  16.3 0.7 compare_reduce_fusion.1
  18.3 0.7 compare_reduce_fusion.4
  23.2 53.2 %collective-permute-done = bf16[128,8192]{1,0:T(8,128)(2,1)} collective-permute-done((bf16[128,8192]{1,0:T(8,128)(2,1)S(1)}, bf16[128,8192]{1,0:T(8,128)(2,1)}, u32[]{:S(2)}, u32[]{:S(2)}) %collective-permute-start) | collective-permute-done | bytes 2097184 | tf_op jit(solution)/shard_map/ppermute | solution.py:16
  76.4 1.8 bitcast_select_fusion
  78.2 1.6 copy.15
  79.8 5.6 %all-to-all-start = ((bf16[128,16,512]{2,0,1:T(8,128)(2,1)}), bf16[128,16,512]{2,0,1:T(8,128)(2,1)}, u32[]{:S(2)}, u32[]{:S(2)}) async-start(bf16[128,16,512]{2,0,1:T(8,128)(2,1)} %bitcast.33), calls=%async_computation | async-start | bytes 4194304 | tf_op jit(solution)/shard_map/all_to_all | solution.py:127
  96.6 102.5 %all_gather.11 = bf16[2048,128]{1,0:T(8,128)(2,1)S(1)} all-gather(bf16[128,128]{1,0:T(8,128)(2,1)S(1)} %fusion.4), channel_id=1, replica_groups=mesh['groups'=2,'fsdp'=16] {'fsdp'}, dimensions={0}, use_global_device_ids=true | all-gather | bytes 557056 | tf_op jit(solution)/shard_map/all_gather | solution.py:128
  199.1 13.4 %fusion.5 = f32[128,8192]{1,0:T(8,128)} fusion(bf16[8192,1024]{1,0:T(8,128)(2,1)} %all-gather.3.cloned.1.call-done, bf16[128,1024]{1,0:T(8,128)(2,1)S(1)} %copy-done.3, pred[128]{0:T(512)(128)(4,1)S(1)} %broadcast_compare_fusion), kind=kOutput, calls=%fused_computation.34 | convolution fusion | flops 2147614720 | bytes 21233792 | tf_op jit(solution)/shard_map/dot_general | solution.py:20
  212.5 26.6 %all-gather.5.cloned.1.call-done = bf16[8192,128]{1,0:T(8,128)(2,1)} async-done(((bf16[512,128]{1,0:T(8,128)(2,1)}), bf16[8192,128]{1,0:T(8,128)(2,1)}) %all-gather.5.cloned.1.call-update) | async-done | bytes 2097168 | tf_op jit(solution)/shard_map/all_gather | solution.py:49
  239.1 5.7 %broadcast_select_fusion.1 = (bf16[128,8192]{1,0:T(8,128)(2,1)}, bf16[128,8192]{1,0:T(8,128)(2,1)}) fusion(pred[]{:T(512)S(6)} %and.43, f32[128,8192]{1,0:T(8,128)} %fusion.5, bf16[128,128]{1,0:T(8,128)(2,1)S(1)} %fusion.4, bf16[8192,128]{1,0:T(8,128)(2,1)} %all-gather.5.cloned.1.call-done), kind=kOutput, calls=%fused_computation.9 | convolution fusion | flops 271581184 | bytes 10518529 | tf_op jit(solution)/shard_map/dot_general | solution.py:20
  244.8 3.2 collective-permute-start.1
  248.0 0.7 fusion.3
  248.7 1.1 convolution_multiply_fusion
  250.1 3.0 fusion.6
  253.1 9.0 %fusion.2 = bf16[128,1024]{1,0:T(8,128)(2,1)} fusion(f32[128,1024]{1,0:T(8,128)S(1)} %convolution_multiply_fusion.1, bf16[128,8192]{1,0:T(8,128)(2,1)S(1)} %bitcast_select_fusion, bf16[8192,1024]{1,0:T(8,128)(2,1)} %all-gather.3.cloned.1.call-done, f32[128]{0:T(128)S(1)} %compare_convert_fusion), kind=kOutput, calls=%fused_computation.14 | convolution fusion | flops 2147876864 | bytes 19661312 | tf_op jit(solution)/shard_map/dot_general | solution.py:52
  262.2 13.4 %collective-permute-done.1 = bf16[128,8192]{1,0:T(8,128)(2,1)} collective-permute-done((bf16[128,8192]{1,0:T(8,128)(2,1)}, bf16[128,8192]{1,0:T(8,128)(2,1)}, u32[]{:S(2)}, u32[]{:S(2)}) %collective-permute-start.1) | collective-permute-done | bytes 2097184 | tf_op jit(solution)/shard_map/ppermute | solution.py:16
  275.6 1.9 select_bitcast_fusion.1
  277.5 2.4 pad_maximum_fusion
  279.9 61.9 %all-reduce.2.cloned.1.call-done = f32[128,1024]{1,0:T(8,128)} async-done(((f32[128,1024]{1,0:T(8,128)}), f32[128,1024]{1,0:T(8,128)}) %all-reduce.2.cloned.1.call-update) | async-done | bytes 524304 | tf_op jit(solution)/shard_map/psum | solution.py:130
  341.7 1.9 copy.17
  (31 shorter events, 4.5 us)
Async XLA Ops:
  7.2 89.1 %copy-start = (bf16[128,1024]{1,0:T(8,128)(2,1)S(1)}, bf16[128,1024]{1,0:T(8,128)(2,1)}, u32[]{:S(2)}) copy-start(bf16[128,1024]{1,0:T(8,128)(2,1)} %param.15) | copy-start | bytes 786436
  7.2 191.9 %all-gather.3.cloned.1.call-start = ((), (), s32[]{:S(2)}) async-start(), calls=%async_computation.1 | async-start | bytes 17825792 | tf_op jit(solution)/shard_map/all_gather | solution.py:51
  7.9 231.2 %all-gather.5.cloned.1.call-start = ((), (), s32[]{:S(2)}) async-start(), calls=%async_computation.2 | async-start | bytes 2228224 | tf_op jit(solution)/shard_map/all_gather | solution.py:49
  11.9 6.3 %copy-start.4 = (s32[32]{0:T(128)S(1)}, s32[32]{0:T(128)}, u32[]{:S(2)}) copy-start(s32[32]{0:T(128)} %param.10) | copy-start | bytes 388
  14.3 62.1 %collective-permute-start = (bf16[128,8192]{1,0:T(8,128)(2,1)S(1)}, bf16[128,8192]{1,0:T(8,128)(2,1)}, u32[]{:S(2)}, u32[]{:S(2)}) collective-permute-start(bf16[128,8192]{1,0:T(8,128)(2,1)S(1)} %select_bitcast_fusion.2), channel_id=1, source_target_pairs={{0,1},{1,2},{2,3},{3,4},{4,5},{5,6},{6,7},{7,8},{8,9},{9,10},{10,1... | collective-permute-start | bytes 6291464 | tf_op jit(solution)/shard_map/ppermute | solution.py:16
  79.8 9.4 %copy-start.5 = (s32[32]{0:T(128)S(1)}, s32[32]{0:T(128)}, u32[]{:S(2)}) copy-start(s32[32]{0:T(128)} %param.12) | copy-start | bytes 388
  79.8 10.0 %copy-start.6 = (s32[32]{0:T(128)S(1)}, s32[32]{0:T(128)}, u32[]{:S(2)}) copy-start(s32[32]{0:T(128)} %param.11) | copy-start | bytes 388
  79.8 16.5 %copy-start.3 = (bf16[128,1024]{1,0:T(8,128)(2,1)S(1)}, bf16[128,1024]{1,0:T(8,128)(2,1)}, u32[]{:S(2)}) copy-start(bf16[128,1024]{1,0:T(8,128)(2,1)} %param.9) | copy-start | bytes 786436
  79.8 170.3 %all-to-all-start = ((bf16[128,16,512]{2,0,1:T(8,128)(2,1)}), bf16[128,16,512]{2,0,1:T(8,128)(2,1)}, u32[]{:S(2)}, u32[]{:S(2)}) async-start(bf16[128,16,512]{2,0,1:T(8,128)(2,1)} %bitcast.33), calls=%async_computation | async-start | bytes 4194304 | tf_op jit(solution)/shard_map/all_to_all | solution.py:127
  85.4 256.3 %all-reduce.2.cloned.1.call-start = ((), (), s32[]{:S(2)}) async-start(), calls=%async_computation.3 | async-start | bytes 1048576 | tf_op jit(solution)/shard_map/psum | solution.py:130
  239.1 8.9 %copy-start.2 = (bf16[8192,128]{1,0:T(8,128)(2,1)S(1)}, bf16[8192,128]{1,0:T(8,128)(2,1)}, u32[]{:S(2)}) copy-start(bf16[8192,128]{1,0:T(8,128)(2,1)} %all-gather.5.cloned.1.call-done) | copy-start | bytes 6291460
  244.8 30.8 %collective-permute-start.1 = (bf16[128,8192]{1,0:T(8,128)(2,1)}, bf16[128,8192]{1,0:T(8,128)(2,1)}, u32[]{:S(2)}, u32[]{:S(2)}) collective-permute-start(bf16[128,8192]{1,0:T(8,128)(2,1)} %get-tuple-element.15), channel_id=1, source_target_pairs={{1,0},{2,1},{3,2},{4,3},{5,4},{6,5},{7,6},{8,7},{9,8},{10,9},{11,1... | collective-permute-start | bytes 6291464 | tf_op jit(solution)/shard_map/ppermute | solution.py:16
  253.1 22.4 %copy-start.1 = (bf16[128,8192]{1,0:T(8,128)(2,1)S(1)}, bf16[128,8192]{1,0:T(8,128)(2,1)}, u32[]{:S(2)}) copy-start(bf16[128,8192]{1,0:T(8,128)(2,1)} %get-tuple-element.16) | copy-start | bytes 6291460
Sparse Core Ops, SparseCore 0:
  10.2 181.7 all-gather.2
  194.2 44.8 all-gather.4
  250.0 91.7 all-reduce.1
where the time goes:
time: 351 us; the launch traced here: 350 us
  waiting for transfers between devices  156 us (44%)
  blocking collectives  103 us (29%)
  matrix products  33.4 us (10%)
  between operations  29 us (8%)
  other arithmetic  13.8 us (4%)
  starting transfers between devices  10.9 us (3%)
  local copies, waits for them, and re-layouts  4.69 us (1%)
    all_gather x1, blocking collectives, body(): every_hidden = lax.all_gather(hidden_state, 'fsdp', axis=0, tiled=True)  103 us
    ppermute x2, waiting for transfers between devices, shifted(): return lax.ppermute(value, axis, pairs)  66.6 us
    psum x1, waiting for transfers between devices, body(): lax.psum(ADAPTER_SCALE * contract_leading(reduced_rank_state, masked_outp...  61.9 us
    all_gather x1, waiting for transfers between devices, adapted_output(): lax.all_gather(adapter_down_weight, 'fsdp', axis=0, tiled=True)  26.6 us
    dot_general x3, matrix products, contract_trailing(): lax.dot_general(left, right, (((1,), (1,)), ((), ())), preferred_element_...  19.3 us
    dot_general x1, matrix products, adapted_output(): jnp.dot(input_rows, piece, preferred_element_type=jnp.float32)  9.04 us
  transfers between devices with their start and end apart: 6, of which 4 were waited for; matrix products, arithmetic and copies ran while one was open for 14% of the time, Pallas kernels for 0%

commit v1 on v0

v1 whole, which is shorter than its diff:
```python
import functools

import jax
import jax.numpy as jnp
from jax import lax
from jax.experimental import pallas as pl
from jax.experimental.pallas import tpu as pltpu
from jax.sharding import PartitionSpec as P

ADAPTER_RANK = 16
BLK = 128
ADAPTER_SCALE = 2.0
REDUCERS = 8
MESH = pl.DeviceIdType.MESH
F32 = jnp.float32
BF16 = jnp.bfloat16


def dot(left, right, left_dim, right_dim):
    return lax.dot_general(
        left, right, (((left_dim,), (right_dim,)), ((), ())), preferred_element_type=F32
    )


def kernel(
    n,
    plan,
    length,
    job,
    codes,
    acts_in,
    cot,
    w_in,
    d_in,
    up,
    values_out,
    grads_out,
    down_out,
    up_out,
    acts,
    wbuf,
    dbuf,
    cot_right,
    dy,
    hidden,
    acc,
    gbuf,
    pbuf,
    pgot,
    ubuf,
    ugot,
    utotal,
    vsend,
    vgot,
    local_sem,
    out_sem,
    cot_sem,
    val_sem,
    w_recv,
    w_send,
    wz_send,
    d_recv,
    d_send,
    dz_send,
    p_send,
    p_recv,
    u_send,
    u_recv,
    t_send,
    t_recv,
):
    nz = n // 4
    rows = w_in.shape[0]
    piece = rows // 4
    tokens = acts.shape[0]
    rank2 = 2 * ADAPTER_RANK
    g = lax.axis_index("groups")
    me = lax.axis_index("fsdp")
    z, y, c = me // 4, (me // 2) % 2, me % 2
    x = g % 2
    to_x = (g + 1 - 2 * x, me)
    to_y = (g, me + 2 - 4 * y)
    to_s = (g, me + 1 - 2 * c)
    to_up = (g, me + 4)
    to_dn = (g, me - 4)

    local = [
        pltpu.make_async_copy(
            w_in, wbuf.at[pl.ds(pl.multiple_of(me * rows, rows), rows)], local_sem.at[0]
        ),
        pltpu.make_async_copy(
            d_in, dbuf.at[pl.ds(pl.multiple_of(me * rows, rows), rows)], local_sem.at[1]
        ),
        pltpu.make_async_copy(acts_in, acts, local_sem.at[2]),
    ]
    for copy in local:
        copy.start()

    barrier = pltpu.get_barrier_semaphore()

    def greet(t, carry):
        pl.semaphore_signal(
            barrier, inc=1, device_id=(g, lax.rem(me + t, n)), device_id_type=MESH
        )
        return carry

    lax.fori_loop(1, n, greet, 0)
    pl.semaphore_signal(barrier, inc=1, device_id=to_x, device_id_type=MESH)
    pl.semaphore_wait(barrier, n)

    def shard_id(z_, y_, c_):
        return z_ * 4 + y_ * 2 + c_

    def w_copy(s, h, q, send, device):
        part = wbuf.at[pl.ds(pl.multiple_of(s * rows + h * 2 * piece + q * piece, piece), piece)]
        return pltpu.make_async_remote_copy(
            src_ref=part,
            dst_ref=part,
            send_sem=send,
            recv_sem=w_recv.at[s * 4 + h * 2 + q],
            device_id=device,
            device_id_type=MESH,
        )

    def d_copy(s, send, device):
        part = dbuf.at[pl.ds(pl.multiple_of(s * rows, rows), rows)]
        return pltpu.make_async_remote_copy(
            src_ref=part,
            dst_ref=part,
            send_sem=send,
            recv_sem=d_recv.at[s],
            device_id=device,
            device_id_type=MESH,
        )

    def w_wait(s, h, q):
        w_copy(s, h, q, w_send.at[0], to_x).wait_recv()

    def d_wait(s):
        d_copy(s, d_send.at[0], to_y).wait_recv()

    cot_copy = pltpu.make_async_remote_copy(
        src_ref=cot,
        dst_ref=cot_right,
        send_sem=cot_sem.at[0],
        recv_sem=cot_sem.at[1],
        device_id=(g, jnp.maximum(me - 1, 0)),
        device_id_type=MESH,
    )

    @pl.when(me > 0)
    def _():
        cot_copy.start()

    local[1].wait()

    @pl.when(z < nz - 1)
    def _():
        d_copy(me, dz_send.at[0], to_up).start()

    @pl.when(z > 0)
    def _():
        d_copy(me, dz_send.at[nz], to_dn).start()

    d_copy(me, d_send.at[0], to_y).start()
    d_copy(me, d_send.at[1], to_s).start()
    local[0].wait()
    for q in range(2):

        @pl.when(z < nz - 1)
        def _():
            w_copy(me, x, q, wz_send.at[q], to_up).start()

        @pl.when(z > 0)
        def _():
            w_copy(me, x, q, wz_send.at[2 * nz + q], to_dn).start()

        w_copy(me, x, q, w_send.at[1], to_y).start()
    for h in range(2):
        for q in range(2):
            w_copy(me, h, q, w_send.at[2], to_s).start()

    @pl.when(me == n - 1)
    def _():
        cot_right[...] = jnp.zeros_like(cot_right)

    @pl.when(me < n - 1)
    def _():
        cot_copy.wait_recv()

    token = lax.broadcasted_iota(jnp.int32, (BLK, 1), 0)
    column = lax.broadcasted_iota(jnp.int32, (BLK, up.shape[0]), 1)
    jobmask = []
    live = []
    for b in range(2):
        p = plan[2 * me + b]
        jobs = job[2 * me + b]
        live.append(token < length[2 * me + b])
        own = live[b] & (p == me)
        right = live[b] & (p == me + 1)
        zero = jnp.zeros((BLK, cot.shape[1]), F32)
        block = jnp.where(
            own,
            cot[...].astype(F32),
            jnp.where(right, cot_right[...].astype(F32), zero),
        ).astype(BF16)
        dy[pl.ds(b * BLK, BLK), :] = block
        jobmask.append((column // ADAPTER_RANK == jobs).astype(F32))
        hidden[pl.ds(b * BLK, BLK), :] = (
            ADAPTER_SCALE * dot(block, up[...], 1, 1) * jobmask[b]
        ).astype(BF16)

    line = lax.broadcasted_iota(jnp.int32, (rank2, up.shape[0]), 0)
    where_col = lax.broadcasted_iota(jnp.int32, (rank2, up.shape[0]), 1)
    line_job = jnp.where(line < ADAPTER_RANK, job[2 * me], job[2 * me + 1])
    pick = (where_col == line_job * ADAPTER_RANK + line % ADAPTER_RANK).astype(F32).astype(BF16)
    same_slot = (
        lax.broadcasted_iota(jnp.int32, (rank2, tokens), 0) // ADAPTER_RANK
        == lax.broadcasted_iota(jnp.int32, (rank2, tokens), 1) // BLK
    )
    hidden_rows = jnp.where(same_slot, dot(pick, hidden[...], 1, 1), 0.0).astype(BF16)
    local[2].wait()

    def cols(s):
        return pl.ds(pl.multiple_of(s * rows, rows), rows)

    def p_part(s, carry):
        pbuf[s] = dot(hidden_rows, acts[:, cols(s)], 1, 0).astype(BF16)
        return carry

    lax.fori_loop(0, n, p_part, 0)

    def p_copy(t):
        other = lax.rem(me + t, n)
        return pltpu.make_async_remote_copy(
            src_ref=pbuf.at[other],
            dst_ref=pgot.at[me],
            send_sem=p_send.at[0],
            recv_sem=p_recv.at[me],
            device_id=(g, other),
            device_id_type=MESH,
        )

    def p_start(t, carry):
        p_copy(t).start()
        return carry

    for d in range(1, nz):

        @pl.when(z >= d)
        def _():
            s = shard_id(z - d, y, c)
            d_wait(s)

            @pl.when(z < nz - 1)
            def _():
                d_copy(s, dz_send.at[d], to_up).start()

            d_copy(s, d_send.at[0], to_y).start()
            d_copy(s, d_send.at[1], to_s).start()

        @pl.when(z + d < nz)
        def _():
            s = shard_id(z + d, y, c)
            d_wait(s)

            @pl.when(z > 0)
            def _():
                d_copy(s, dz_send.at[nz + d], to_dn).start()

            d_copy(s, d_send.at[0], to_y).start()
            d_copy(s, d_send.at[1], to_s).start()

    lax.fori_loop(1, n, p_start, 0)
    pgot[me] = pbuf[me]

    def z_part(d):
        for up_way in (True, False):

            @pl.when(z >= d if up_way else z + d < nz)
            def _():
                s = shard_id(z - d if up_way else z + d, y, c)
                for q in range(2):
                    w_wait(s, x, q)

                    @pl.when(z < nz - 1 if up_way else z > 0)
                    def _():
                        w_copy(
                            s,
                            x,
                            q,
                            wz_send.at[(0 if up_way else 2 * nz) + 2 * d + q],
                            to_up if up_way else to_dn,
                        ).start()

                    w_copy(s, x, q, w_send.at[0], to_x).start()
                    w_copy(s, x, q, w_send.at[1], to_y).start()
                    w_copy(s, x, q, w_send.at[2], to_s).start()

    def xy_part(d):
        for up_way in (True, False):

            @pl.when(z >= d if up_way else z + d < nz)
            def _():
                z_ = z - d if up_way else z + d
                a = shard_id(z_, y, c)
                b = shard_id(z_, 1 - y, c)
                for q in range(2):
                    w_wait(a, 1 - x, q)
                    if q == 0:
                        w_copy(a, 1 - x, q, w_send.at[1], to_y).start()
                    w_copy(a, 1 - x, q, w_send.at[2], to_s).start()
                    w_wait(b, x, q)
                    if q == 1:
                        w_copy(b, x, q, w_send.at[0], to_x).start()
                    w_copy(b, x, q, w_send.at[2], to_s).start()
                for q in range(2):
                    w_wait(b, 1 - x, q)
                    w_copy(b, 1 - x, q, w_send.at[2], to_s).start()

    first = shard_id(z, 1 - y, c)
    for q in range(2):
        w_wait(first, x, q)
        w_copy(first, x, q, w_send.at[0], to_x).start()
        w_copy(first, x, q, w_send.at[2], to_s).start()

    for z_ in range(nz):
        s = shard_id(z_, 1 - y, c)
        d_wait(s)
        d_copy(s, d_send.at[1], to_s).start()

    def d_sib(i, carry):
        d_wait(2 * i + 1 - c)
        return carry

    lax.fori_loop(0, n // 2, d_sib, 0)

    acc[...] = jnp.zeros_like(acc)

    def low_part(s, total):
        return total + dot(acts[:, cols(s)], dbuf[cols(s), :], 1, 0)

    low = lax.fori_loop(0, n, low_part, jnp.zeros((tokens, up.shape[0]), F32))
    low = (low * jnp.concatenate(jobmask, 0)).astype(BF16)
    low_rows = jnp.where(same_slot, dot(pick, low, 1, 1), 0.0).astype(BF16)
    up_part = (ADAPTER_SCALE * dot(low_rows, dy[...], 1, 0)).astype(BF16)
    width = up_part.shape[1] // REDUCERS
    every = n // REDUCERS
    for k in range(REDUCERS):
        ubuf[k] = up_part[:, k * width : (k + 1) * width]
    for k in range(REDUCERS):

        @pl.when(me == k * every)
        def _():
            ugot[me] = ubuf[k]

        @pl.when(me != k * every)
        def _():
            pltpu.make_async_remote_copy(
                src_ref=ubuf.at[k],
                dst_ref=ugot.at[me],
                send_sem=u_send.at[k],
                recv_sem=u_recv.at[me],
                device_id=(g, k * every),
                device_id_type=MESH,
            ).start()

    def compute(s):
        a = acts[:, cols(s)]
        w = wbuf[cols(s), :]
        acc[...] += dot(a, w, 1, 0)
        gbuf[:, cols(s)] = (dot(dy[...], w, 1, 1) + dot(hidden[...], dbuf[cols(s), :], 1, 1)).astype(BF16)
        pltpu.make_async_copy(gbuf.at[:, cols(s)], grads_out.at[:, cols(s)], out_sem.at[0]).start()

    def slab(d, ways):
        def one(i, carry):
            down_way, j = i // 4, i % 4
            z_ = jnp.where(down_way == 1, z + d, z - d)
            y_ = lax.rem(y + j, 2)
            c_ = lax.rem(c + j // 2, 2)

            @pl.when((z_ >= 0) & (z_ < nz))
            def _():
                s = shard_id(z_, y_, c_)

                @pl.when(c_ != c)
                def _():
                    for h in range(2):
                        for q in range(2):
                            w_wait(s, h, q)

                compute(s)

            return carry

        lax.fori_loop(0, 4 * ways, one, 0)

    if nz > 1:
        z_part(1)
    for q in range(2):
        w_wait(first, 1 - x, q)
        w_copy(first, 1 - x, q, w_send.at[2], to_s).start()
    slab(0, 1)

    def t_copy(k, other):
        return pltpu.make_async_remote_copy(
            src_ref=utotal.at[k],
            dst_ref=utotal.at[k],
            send_sem=t_send.at[0],
            recv_sem=t_recv.at[k],
            device_id=(g, other),
            device_id_type=MESH,
        )

    hot = (
        lax.broadcasted_iota(jnp.int32, (up.shape[0], codes.shape[1]), 0) == codes[...]
    ).astype(F32).astype(BF16)

    @pl.when(me % every == 0)
    def _():
        def u_wait(t, carry):
            other = lax.rem(me + t, n)
            pltpu.make_async_remote_copy(
                src_ref=ubuf.at[0],
                dst_ref=ugot.at[other],
                send_sem=u_send.at[0],
                recv_sem=u_recv.at[other],
                device_id=(g, other),
                device_id_type=MESH,
            ).wait_recv()
            return carry

        lax.fori_loop(1, n, u_wait, 0)
        k = me // every
        utotal[k] = dot(hot, ugot[...].reshape(n * rank2, width), 1, 0).astype(BF16)

        def t_start(t, carry):
            t_copy(k, lax.rem(me + t, n)).start()
            return carry

        lax.fori_loop(1, n, t_start, 0)

    def p_wait(t, carry):
        other = lax.rem(me + t, n)
        pltpu.make_async_remote_copy(
            src_ref=pbuf.at[0],
            dst_ref=pgot.at[other],
            send_sem=p_send.at[0],
            recv_sem=p_recv.at[other],
            device_id=(g, other),
            device_id_type=MESH,
        ).wait_recv()
        return carry

    lax.fori_loop(1, n, p_wait, 0)
    down_out[...] = dot(pgot[...].reshape(n * rank2, rows), hot, 0, 1)

    def step(d, carry):
        @pl.when(d + 1 < nz)
        def _():
            z_part(d + 1)

        xy_part(d)
        slab(d, 2)
        return carry

    lax.fori_loop(1, nz, step, 0)

    whole = acc[...] + ADAPTER_SCALE * dot(low, up[...], 1, 0)
    keep = jnp.zeros((BLK, up.shape[1]), F32)
    give = keep
    for b in range(2):
        p = plan[2 * me + b]
        block = whole[b * BLK : (b + 1) * BLK]
        keep = jnp.where(live[b] & (p == me), block, keep)
        give = jnp.where(live[b] & (p == me + 1), block, give)
    vsend[...] = give.astype(BF16)
    val_copy = pltpu.make_async_remote_copy(
        src_ref=vsend,
        dst_ref=vgot,
        send_sem=val_sem.at[0],
        recv_sem=val_sem.at[1],
        device_id=(g, jnp.minimum(me + 1, n - 1)),
        device_id_type=MESH,
    )

    @pl.when(me < n - 1)
    def _():
        val_copy.start()

    for k in range(REDUCERS):

        @pl.when(me != k * every)
        def _():
            t_copy(k, k * every).wait_recv()

        up_out[:, k * width : (k + 1) * width] = utotal[k].astype(F32)

    def drain(ref, sem):
        pltpu.make_async_copy(ref, ref, sem).wait()

    drain(wbuf.at[pl.ds(0, (3 * nz - 1) * piece)], w_send.at[0])
    drain(wbuf.at[pl.ds(0, (3 * nz - 1) * piece)], w_send.at[1])
    drain(wbuf.at[pl.ds(0, n // 2 * rows)], w_send.at[2])
    drain(dbuf.at[pl.ds(0, nz * rows)], d_send.at[0])
    drain(dbuf.at[pl.ds(0, n // 2 * rows)], d_send.at[1])
    drain(pbuf.at[pl.ds(0, n - 1)], p_send.at[0])

    for d in range(nz):
        for up_way in (True, False):

            @pl.when((z >= d) & (z < nz - 1) if up_way else (z + d < nz) & (z > 0))
            def _():
                s = shard_id(z - d if up_way else z + d, y, c)
                base = 0 if up_way else nz
                d_copy(s, dz_send.at[base + d], to_y).wait_send()
                for q in range(2):
                    w_copy(s, x, q, wz_send.at[2 * base + 2 * d + q], to_y).wait_send()

    for k in range(REDUCERS):

        @pl.when(me != k * every)
        def _():
            drain(ubuf.at[k], u_send.at[k])

    @pl.when(me % every == 0)
    def _():
        drain(dbuf.at[pl.ds(0, (n - 1) * width)], t_send.at[0])

    @pl.when(me > 0)
    def _():
        cot_copy.wait_send()

    pltpu.make_async_copy(gbuf, grads_out, out_sem.at[0]).wait()

    @pl.when(me < n - 1)
    def _():
        val_copy.wait_send()

    @pl.when(me == 0)
    def _():
        values_out[...] = keep.astype(BF16)

    @pl.when(me > 0)
    def _():
        val_copy.wait_recv()
        values_out[...] = (keep + vgot[...].astype(F32)).astype(BF16)


def body(
    n,
    acts,
    cotangent,
    plan,
    source_block_length,
    source_block_job,
    frozen_value_weight,
    adapter_down_weight,
    adapter_up_weight,
):
    tokens, features = acts.shape
    rows, out_width = frozen_value_weight.shape
    job_columns = adapter_down_weight.shape[1]
    rank2 = 2 * ADAPTER_RANK
    width = out_width // REDUCERS
    codes = (
        source_block_job[:, None] * ADAPTER_RANK + jnp.arange(ADAPTER_RANK, dtype=jnp.int32)[None]
    ).reshape(1, -1)
    smem = pl.BlockSpec(memory_space=pltpu.SMEM)
    vmem = pl.BlockSpec(memory_space=pltpu.VMEM)
    anywhere = pl.BlockSpec(memory_space=pl.ANY)
    dma = pltpu.SemaphoreType.DMA
    nz = n // 4
    return pl.pallas_call(
        functools.partial(kernel, n),
        out_shape=(
            jax.ShapeDtypeStruct((BLK, out_width), BF16),
            jax.ShapeDtypeStruct((tokens, features), BF16),
            jax.ShapeDtypeStruct((rows, job_columns), F32),
            jax.ShapeDtypeStruct((job_columns, out_width), F32),
        ),
        in_specs=[smem, smem, smem, vmem, anywhere, vmem, anywhere, anywhere, vmem],
        out_specs=(vmem, anywhere, vmem, vmem),
        scratch_shapes=[
            pltpu.VMEM((tokens, features), BF16),
            pltpu.VMEM((n * rows, out_width), BF16),
            pltpu.VMEM((n * rows, job_columns), BF16),
            pltpu.VMEM((BLK, out_width), BF16),
            pltpu.VMEM((tokens, out_width), BF16),
            pltpu.VMEM((tokens, job_columns), BF16),
            pltpu.VMEM((tokens, out_width), F32),
            pltpu.VMEM((tokens, features), BF16),
            pltpu.VMEM((n, rank2, rows), BF16),
            pltpu.VMEM((n, rank2, rows), BF16),
            pltpu.VMEM((REDUCERS, rank2, width), BF16),
            pltpu.VMEM((n, rank2, width), BF16),
            pltpu.VMEM((REDUCERS, job_columns, width), BF16),
            pltpu.VMEM((BLK, out_width), BF16),
            pltpu.VMEM((BLK, out_width), BF16),
            dma((3,)),
            dma((1,)),
            dma((2,)),
            dma((2,)),
            dma((n * 4,)),
            dma((3,)),
            dma((4 * nz,)),
            dma((n,)),
            dma((2,)),
            dma((2 * nz,)),
            dma((1,)),
            dma((n,)),
            dma((REDUCERS,)),
            dma((n,)),
            dma((1,)),
            dma((REDUCERS,)),
        ],
        compiler_params=pltpu.CompilerParams(
            collective_id=0, has_side_effects=True, vmem_limit_bytes=56 * 1024 * 1024
        ),
        cost_estimate=pl.CostEstimate(
            flops=4 * tokens * features * out_width,
            bytes_accessed=4 * tokens * features,
            transcendentals=0,
        ),
    )(
        plan,
        source_block_length,
        source_block_job,
        codes,
        acts,
        cotangent,
        frozen_value_weight,
        adapter_down_weight,
        adapter_up_weight,
    )


def solution(mesh):
    placed = (
        P(("groups", "fsdp"), None),
        P(("groups", "fsdp"), None),
        P("groups"),
        P("groups"),
        P("groups"),
        P("fsdp", None),
        P(("groups", "fsdp"), None),
        P("groups", None),
    )
    return jax.shard_map(
        functools.partial(body, mesh.shape["fsdp"]),
        mesh=mesh,
        in_specs=placed,
        out_specs=(
            P(("groups", "fsdp"), None),
            P(("groups", "fsdp"), None),
            P(("groups", "fsdp"), None),
            P("groups", None),
        ),
        check_vma=False,
    )
```

time: 351 us -> 131 us (0.37)
  waiting for transfers between devices: 156 us -> 0 us
  Pallas kernels: 0 us -> 121 us
  blocking collectives: 103 us -> 0 us
  matrix products: 33.4 us -> 0 us
  between operations: 29 us -> 0.64 us
  other arithmetic: 13.8 us -> 0.73 us
  starting transfers between devices: 10.9 us -> 0 us
  local copies, waits for them, and re-layouts: 4.69 us -> 8.55 us
    pallas_call x0 -> x1, Pallas kernels: none -> 121 us  [body(): pl.pallas_call(functools.partial(kernel, n), out_shape=(jax.ShapeDtypeStr...]
    all_gather x1 -> x0, blocking collectives: 103 us -> none  [body(): every_hidden = lax.all_gather(hidden_state, 'fsdp', axis=0, tiled=True)]
    ppermute x2 -> x0, waiting for transfers between devices: 66.6 us -> none  [shifted(): return lax.ppermute(value, axis, pairs)]
    psum x1 -> x0, waiting for transfers between devices: 61.9 us -> none  [body(): lax.psum(ADAPTER_SCALE * contract_leading(reduced_rank_state, masked_outp...]
    dot_general x8 -> x0, matrix products: 33.4 us -> none  [the longest x3 19.3 us: contract_trailing(): lax.dot_general(left, right, (((1,), (1,)), ((), ())), preferred_element_...]
    all_gather x2 -> x0, waiting for transfers between devices: 26.6 us -> none  [the longest x1 26.6 us: adapted_output(): lax.all_gather(adapter_down_weight, 'fsdp', axis=0, tiled=True)]
    another operation x5 -> x0, other arithmetic: 6.3 us -> none  [the longest x2 4.31 us: body(): jnp.stack(grad_slots, 0).reshape(slot_count * BLK, feature_width)]
    unnamed x15 -> x8, local copies, waits for them, and re-layouts: 1.92 us -> 7.88 us
  transfers between devices with their start and end apart: 6 -> 0, of which waited for: 4 -> 0; matrix products, arithmetic and copies ran while one was open for 14% -> 0% of each run, Pallas kernels for 0% -> 0%
where the time goes in v1:
time: 131 us
  Pallas kernels  121 us (92%)
  local copies, waits for them, and re-layouts  8.55 us (7%)
    pallas_call x1, Pallas kernels, body(): pl.pallas_call(functools.partial(kernel, n), out_shape=(jax.ShapeDtypeStr...  121 us
    unnamed x8, local copies, waits for them, and re-layouts  7.88 us

profile of v1, /device:TPU:8, one launch (start us, length us, event | category | flops | bytes accessed | tf_op | source)
XLA Modules:
  0.0 130.9 jit_solution(1765674228963523489)
XLA Ops:
  0.6 0.7 broadcast_multiply_fusion
  1.3 0.1 iota_add_fusion
  1.4 0.7 add.26.codes
  2.0 121.0 %shard_map.111 = (bf16[128,1024]{1,0:T(8,128)(2,1)}, bf16[256,8192]{1,0:T(8,128)(2,1)}, f32[512,128]{1,0:T(8,128)}, f32[128,1024]{1,0:T(8,128)}) custom-call(s32[32]{0:T(128)} %plan.1, s32[32]{0:T(128)} %length.1, s32[32]{0:T(128)} %job.1, s32[1,512]{1,0:T(1,128)} %add.26.codes, bf16[256,8192]{1,0:T(8,128)(2,1)} %acts_in.1, bf16[128,1024]{1,0:T(8,128)(2,1)} %cot.1, ...), custom_call_target="tpu_custom_call" | custom-call | flops 8589934592 | bytes 8388608 | tf_op jit(solution)/shard_map/pallas_call | solution.py:574
  123.0 1.7 %copy.16 = bf16[128,1024]{1,0:T(8,128)(2,1)} copy(bf16[128,1024]{1,0:T(8,128)(2,1)} %get-tuple-element.8) | data formatting | bytes 524288
  124.7 0.0 copy-start.1
  124.7 0.0 copy-start
  124.7 4.7 %copy.17 = bf16[256,8192]{1,0:T(8,128)(2,1)} copy(bf16[256,8192]{1,0:T(8,128)(2,1)} %get-tuple-element.9) | data formatting | bytes 8388608
  129.4 0.0 copy-done.1
  129.4 0.7 copy.18
  130.1 0.0 copy-done
  130.1 0.8 copy.19
Async XLA Ops:
  124.7 4.7 %copy-start.1 = (f32[512,128]{1,0:T(8,128)S(1)}, f32[512,128]{1,0:T(8,128)}, u32[]{:S(2)}) copy-start(f32[512,128]{1,0:T(8,128)} %get-tuple-element.10) | copy-start | bytes 786436
  124.7 5.4 %copy-start = (f32[128,1024]{1,0:T(8,128)S(1)}, f32[128,1024]{1,0:T(8,128)}, u32[]{:S(2)}) copy-start(f32[128,1024]{1,0:T(8,128)} %get-tuple-element.11) | copy-start | bytes 1572868

commit v2 on v1

--- a/solution.py
+++ b/solution.py
@@ -34,17 +34,17 @@
     d_in,
     up,
     values_out,
-    grads_out,
+    gbuf,
     down_out,
     up_out,
     acts,
     wbuf,
-    dbuf,
+    dsend,
+    dgot,
     cot_right,
     dy,
     hidden,
     acc,
-    gbuf,
     pbuf,
     pgot,
     ubuf,
@@ -53,7 +53,6 @@
     vsend,
     vgot,
     local_sem,
-    out_sem,
     cot_sem,
     val_sem,
     w_recv,
@@ -61,7 +60,6 @@
     wz_send,
     d_recv,
     d_send,
-    dz_send,
     p_send,
     p_recv,
     u_send,
@@ -88,10 +86,7 @@
         pltpu.make_async_copy(
             w_in, wbuf.at[pl.ds(pl.multiple_of(me * rows, rows), rows)], local_sem.at[0]
         ),
-        pltpu.make_async_copy(
-            d_in, dbuf.at[pl.ds(pl.multiple_of(me * rows, rows), rows)], local_sem.at[1]
-        ),
-        pltpu.make_async_copy(acts_in, acts, local_sem.at[2]),
+        pltpu.make_async_copy(acts_in, acts, local_sem.at[1]),
     ]
     for copy in local:
         copy.start()
@@ -122,22 +117,8 @@
             device_id_type=MESH,
         )
 
-    def d_copy(s, send, device):
-        part = dbuf.at[pl.ds(pl.multiple_of(s * rows, rows), rows)]
-        return pltpu.make_async_remote_copy(
-            src_ref=part,
-            dst_ref=part,
-            send_sem=send,
-            recv_sem=d_recv.at[s],
-            device_id=device,
-            device_id_type=MESH,
-        )
-
     def w_wait(s, h, q):
         w_copy(s, h, q, w_send.at[0], to_x).wait_recv()
-
-    def d_wait(s):
-        d_copy(s, d_send.at[0], to_y).wait_recv()
 
     cot_copy = pltpu.make_async_remote_copy(
         src_ref=cot,
@@ -152,18 +133,6 @@
     def _():
         cot_copy.start()
 
-    local[1].wait()
-
-    @pl.when(z < nz - 1)
-    def _():
-        d_copy(me, dz_send.at[0], to_up).start()
-
-    @pl.when(z > 0)
-    def _():
-        d_copy(me, dz_send.at[nz], to_dn).start()
-
-    d_copy(me, d_send.at[0], to_y).start()
-    d_copy(me, d_send.at[1], to_s).start()
     local[0].wait()
     for q in range(2):
 
@@ -179,6 +148,56 @@
     for h in range(2):
         for q in range(2):
             w_copy(me, h, q, w_send.at[2], to_s).start()
+
+    hot = (
+        lax.broadcasted_iota(jnp.int32, (up.shape[0], codes.shape[1]), 0) == codes[...]
+    ).astype(F32).astype(BF16)
+
+    def cols(s):
+        return pl.ds(pl.multiple_of(s * rows, rows), rows)
+
+    dsend[...] = dot(hot, d_in[...], 0, 1).astype(BF16).reshape(n, rank2, rows)
+    dgot[me] = dsend[me]
+
+    def exchange(src, dst, send, recv, t):
+        other = lax.rem(me + t, n)
+        return pltpu.make_async_remote_copy(
+            src_ref=src.at[other],
+            dst_ref=dst.at[me],
+            send_sem=send.at[0],
+            recv_sem=recv.at[me],
+            device_id=(g, other),
+            device_id_type=MESH,
+        )
+
+    def arrived(src, dst, send, recv, t):
+        other = lax.rem(me + t, n)
+        pltpu.make_async_remote_copy(
+            src_ref=src.at[0],
+            dst_ref=dst.at[other],
+            send_sem=send.at[0],
+            recv_sem=recv.at[other],
+            device_id=(g, other),
+            device_id_type=MESH,
+        ).wait_recv()
+
+    def d_start(t, carry):
+        exchange(dsend, dgot, d_send, d_recv, t).start()
+        return carry
+
+    def d_wait(t, carry):
+        arrived(dsend, dgot, d_send, d_recv, t)
+        return carry
+
+    def p_start(t, carry):
+        exchange(pbuf, pgot, p_send, p_recv, t).start()
+        return carry
+
+    def p_wait(t, carry):
+        arrived(pbuf, pgot, p_send, p_recv, t)
+        return carry
+
+    lax.fori_loop(1, n, d_start, 0)
 
     @pl.when(me == n - 1)
     def _():
@@ -219,10 +238,7 @@
         == lax.broadcasted_iota(jnp.int32, (rank2, tokens), 1) // BLK
     )
     hidden_rows = jnp.where(same_slot, dot(pick, hidden[...], 1, 1), 0.0).astype(BF16)
-    local[2].wait()
-
-    def cols(s):
-        return pl.ds(pl.multiple_of(s * rows, rows), rows)
+    local[1].wait()
 
     def p_part(s, carry):
         pbuf[s] = dot(hidden_rows, acts[:, cols(s)], 1, 0).astype(BF16)
@@ -230,48 +246,6 @@
 
     lax.fori_loop(0, n, p_part, 0)
 
-    def p_copy(t):
-        other = lax.rem(me + t, n)
-        return pltpu.make_async_remote_copy(
-            src_ref=pbuf.at[other],
-            dst_ref=pgot.at[me],
-            send_sem=p_send.at[0],
-            recv_sem=p_recv.at[me],
-            device_id=(g, other),
-            device_id_type=MESH,
-        )
-
-    def p_start(t, carry):
-        p_copy(t).start()
-        return carry
-
-    for d in range(1, nz):
-
-        @pl.when(z >= d)
-        def _():
-            s = shard_id(z - d, y, c)
-            d_wait(s)
-
-            @pl.when(z < nz - 1)
-            def _():
-                d_copy(s, dz_send.at[d], to_up).start()
-
-            d_copy(s, d_send.at[0], to_y).start()
-            d_copy(s, d_send.at[1], to_s).start()
-
-        @pl.when(z + d < nz)
-        def _():
-            s = shard_id(z + d, y, c)
-            d_wait(s)
-
-            @pl.when(z > 0)
-            def _():
-                d_copy(s, dz_send.at[nz + d], to_dn).start()
-
-            d_copy(s, d_send.at[0], to_y).start()
-            d_copy(s, d_send.at[1], to_s).start()
-
-    lax.fori_loop(1, n, p_start, 0)
     pgot[me] = pbuf[me]
 
     def z_part(d):
@@ -318,31 +292,56 @@
                     w_wait(b, 1 - x, q)
                     w_copy(b, 1 - x, q, w_send.at[2], to_s).start()
 
+    acc[...] = jnp.zeros_like(acc)
+
+    def compute(s):
+        a = acts[:, cols(s)]
+        w = wbuf[cols(s), :]
+        acc[...] += dot(a, w, 1, 0)
+        gbuf[:, cols(s)] = (dot(dy[...], w, 1, 1) + dot(hidden_rows, dgot[s], 0, 0)).astype(BF16)
+
+    def slab(d, ways):
+        def one(i, carry):
+            down_way, j = i // 4, i % 4
+            z_ = jnp.where(down_way == 1, z + d, z - d)
+            y_ = lax.rem(y + j, 2)
+            c_ = lax.rem(c + j // 2, 2)
+
+            @pl.when((z_ >= 0) & (z_ < nz))
+            def _():
+                s = shard_id(z_, y_, c_)
+
+                @pl.when(c_ != c)
+                def _():
+                    for h in range(2):
+                        for q in range(2):
+                            w_wait(s, h, q)
+
+                compute(s)
+
+            return carry
+
+        lax.fori_loop(0, 4 * ways, one, 0)
+
     first = shard_id(z, 1 - y, c)
     for q in range(2):
         w_wait(first, x, q)
         w_copy(first, x, q, w_send.at[0], to_x).start()
         w_copy(first, x, q, w_send.at[2], to_s).start()
 
-    for z_ in range(nz):
-        s = shard_id(z_, 1 - y, c)
-        d_wait(s)
-        d_copy(s, d_send.at[1], to_s).start()
-
-    def d_sib(i, carry):
-        d_wait(2 * i + 1 - c)
-        return carry
-
-    lax.fori_loop(0, n // 2, d_sib, 0)
-
-    acc[...] = jnp.zeros_like(acc)
+    if nz > 1:
+        z_part(1)
+    for q in range(2):
+        w_wait(first, 1 - x, q)
+        w_copy(first, 1 - x, q, w_send.at[2], to_s).start()
+
+    lax.fori_loop(1, n, d_wait, 0)
 
     def low_part(s, total):
-        return total + dot(acts[:, cols(s)], dbuf[cols(s), :], 1, 0)
-
-    low = lax.fori_loop(0, n, low_part, jnp.zeros((tokens, up.shape[0]), F32))
-    low = (low * jnp.concatenate(jobmask, 0)).astype(BF16)
-    low_rows = jnp.where(same_slot, dot(pick, low, 1, 1), 0.0).astype(BF16)
+        return total + dot(dgot[s], acts[:, cols(s)], 1, 1)
+
+    low = lax.fori_loop(0, n, low_part, jnp.zeros((rank2, tokens), F32))
+    low_rows = jnp.where(same_slot, low, 0.0).astype(BF16)
     up_part = (ADAPTER_SCALE * dot(low_rows, dy[...], 1, 0)).astype(BF16)
     width = up_part.shape[1] // REDUCERS
     every = n // REDUCERS
@@ -365,41 +364,6 @@
                 device_id_type=MESH,
             ).start()
 
-    def compute(s):
-        a = acts[:, cols(s)]
-        w = wbuf[cols(s), :]
-        acc[...] += dot(a, w, 1, 0)
-        gbuf[:, cols(s)] = (dot(dy[...], w, 1, 1) + dot(hidden[...], dbuf[cols(s), :], 1, 1)).astype(BF16)
-        pltpu.make_async_copy(gbuf.at[:, cols(s)], grads_out.at[:, cols(s)], out_sem.at[0]).start()
-
-    def slab(d, ways):
-        def one(i, carry):
-            down_way, j = i // 4, i % 4
-            z_ = jnp.where(down_way == 1, z + d, z - d)
-            y_ = lax.rem(y + j, 2)
-            c_ = lax.rem(c + j // 2, 2)
-
-            @pl.when((z_ >= 0) & (z_ < nz))
-            def _():
-                s = shard_id(z_, y_, c_)
-
-                @pl.when(c_ != c)
-                def _():
-                    for h in range(2):
-                        for q in range(2):
-                            w_wait(s, h, q)
-
-                compute(s)
-
-            return carry
-
-        lax.fori_loop(0, 4 * ways, one, 0)
-
-    if nz > 1:
-        z_part(1)
-    for q in range(2):
-        w_wait(first, 1 - x, q)
-        w_copy(first, 1 - x, q, w_send.at[2], to_s).start()
     slab(0, 1)
 
     def t_copy(k, other):
@@ -412,12 +376,7 @@
             device_id_type=MESH,
         )
 
-    hot = (
-        lax.broadcasted_iota(jnp.int32, (up.shape[0], codes.shape[1]), 0) == codes[...]
-    ).astype(F32).astype(BF16)
-
-    @pl.when(me % every == 0)
-    def _():
+    def reduce_up():
         def u_wait(t, carry):
             other = lax.rem(me + t, n)
             pltpu.make_async_remote_copy(
@@ -440,33 +399,29 @@
 
         lax.fori_loop(1, n, t_start, 0)
 
-    def p_wait(t, carry):
-        other = lax.rem(me + t, n)
-        pltpu.make_async_remote_copy(
-            src_ref=pbuf.at[0],
-            dst_ref=pgot.at[other],
-            send_sem=p_send.at[0],
-            recv_sem=p_recv.at[other],
-            device_id=(g, other),
-            device_id_type=MESH,
-        ).wait_recv()
-        return carry
-
-    lax.fori_loop(1, n, p_wait, 0)
-    down_out[...] = dot(pgot[...].reshape(n * rank2, rows), hot, 0, 1)
-
     def step(d, carry):
         @pl.when(d + 1 < nz)
         def _():
             z_part(d + 1)
 
+        @pl.when(d == nz - 2)
+        def _():
+            lax.fori_loop(1, n, p_start, 0)
+
         xy_part(d)
+
+        @pl.when((d == nz - 1) & (me % every == 0))
+        def _():
+            reduce_up()
+
         slab(d, 2)
         return carry
 
     lax.fori_loop(1, nz, step, 0)
 
-    whole = acc[...] + ADAPTER_SCALE * dot(low, up[...], 1, 0)
+
+    up_rows = dot(pick, up[...], 1, 0).astype(BF16)
+    whole = acc[...] + ADAPTER_SCALE * dot(low_rows, up_rows, 0, 0)
     keep = jnp.zeros((BLK, up.shape[1]), F32)
     give = keep
     for b in range(2):
@@ -488,6 +443,9 @@
     def _():
         val_copy.start()
 
+    lax.fori_loop(1, n, p_wait, 0)
+    down_out[...] = dot(pgot[...].reshape(n * rank2, rows), hot, 0, 1)
+
     for k in range(REDUCERS):
 
         @pl.when(me != k * every)
@@ -502,8 +460,7 @@
     drain(wbuf.at[pl.ds(0, (3 * nz - 1) * piece)], w_send.at[0])
     drain(wbuf.at[pl.ds(0, (3 * nz - 1) * piece)], w_send.at[1])
     drain(wbuf.at[pl.ds(0, n // 2 * rows)], w_send.at[2])
-    drain(dbuf.at[pl.ds(0, nz * rows)], d_send.at[0])
-    drain(dbuf.at[pl.ds(0, n // 2 * rows)], d_send.at[1])
+    drain(dsend.at[pl.ds(0, n - 1)], d_send.at[0])
     drain(pbuf.at[pl.ds(0, n - 1)], p_send.at[0])
 
     for d in range(nz):
@@ -513,7 +470,6 @@
             def _():
                 s = shard_id(z - d if up_way else z + d, y, c)
                 base = 0 if up_way else nz
-                d_copy(s, dz_send.at[base + d], to_y).wait_send()
                 for q in range(2):
                     w_copy(s, x, q, wz_send.at[2 * base + 2 * d + q], to_y).wait_send()
 
@@ -525,13 +481,12 @@
 
     @pl.when(me % every == 0)
     def _():
-        drain(dbuf.at[pl.ds(0, (n - 1) * width)], t_send.at[0])
+        drain(wbuf.at[pl.ds(0, (n - 1) * up.shape[0] // REDUCERS)], t_send.at[0])
 
     @pl.when(me > 0)
     def _():
         cot_copy.wait_send()
 
-    pltpu.make_async_copy(gbuf, grads_out, out_sem.at[0]).wait()
 
     @pl.when(me < n - 1)
     def _():
@@ -575,21 +530,21 @@
         functools.partial(kernel, n),
         out_shape=(
             jax.ShapeDtypeStruct((BLK, out_width), BF16),
-            jax.ShapeDtypeStruct((tokens, features), BF16),
+            pltpu.VMEM((tokens, features), BF16),
             jax.ShapeDtypeStruct((rows, job_columns), F32),
             jax.ShapeDtypeStruct((job_columns, out_width), F32),
         ),
-        in_specs=[smem, smem, smem, vmem, anywhere, vmem, anywhere, anywhere, vmem],
-        out_specs=(vmem, anywhere, vmem, vmem),
+        in_specs=[smem, smem, smem, vmem, anywhere, vmem, anywhere, vmem, vmem],
+        out_specs=(vmem, vmem, vmem, vmem),
         scratch_shapes=[
             pltpu.VMEM((tokens, features), BF16),
             pltpu.VMEM((n * rows, out_width), BF16),
-            pltpu.VMEM((n * rows, job_columns), BF16),
+            pltpu.VMEM((n, rank2, rows), BF16),
+            pltpu.VMEM((n, rank2, rows), BF16),
             pltpu.VMEM((BLK, out_width), BF16),
             pltpu.VMEM((tokens, out_width), BF16),
             pltpu.VMEM((tokens, job_columns), BF16),
             pltpu.VMEM((tokens, out_width), F32),
-            pltpu.VMEM((tokens, features), BF16),
             pltpu.VMEM((n, rank2, rows), BF16),
             pltpu.VMEM((n, rank2, rows), BF16),
             pltpu.VMEM((REDUCERS, rank2, width), BF16),
@@ -597,16 +552,14 @@
             pltpu.VMEM((REDUCERS, job_columns, width), BF16),
             pltpu.VMEM((BLK, out_width), BF16),
             pltpu.VMEM((BLK, out_width), BF16),
-            dma((3,)),
-            dma((1,)),
+            dma((2,)),
             dma((2,)),
             dma((2,)),
             dma((n * 4,)),
             dma((3,)),
             dma((4 * nz,)),
             dma((n,)),
-            dma((2,)),
-            dma((2 * nz,)),
+            dma((1,)),
             dma((1,)),
             dma((n,)),
             dma((REDUCERS,)),
@@ -615,7 +568,7 @@
             dma((REDUCERS,)),
         ],
         compiler_params=pltpu.CompilerParams(
-            collective_id=0, has_side_effects=True, vmem_limit_bytes=56 * 1024 * 1024
+            collective_id=0, has_side_effects=True, vmem_limit_bytes=57 * 1024 * 1024
         ),
         cost_estimate=pl.CostEstimate(
             flops=4 * tokens * features * out_width,

time: 131 us -> 115 us (0.88)
  Pallas kernels: 121 us -> 108 us
  local copies, waits for them, and re-layouts: 8.55 us -> 4.89 us
    pallas_call x1, Pallas kernels: 121 us -> 108 us  [body(): pl.pallas_call(functools.partial(kernel, n), out_shape=(jax.ShapeDtypeStr...]
    unnamed x8 -> x10, local copies, waits for them, and re-layouts: 7.88 us -> 4.23 us
where the time goes in v2:
time: 115 us
  Pallas kernels  108 us (94%)
  local copies, waits for them, and re-layouts  4.89 us (4%)
    pallas_call x1, Pallas kernels, body(): pl.pallas_call(functools.partial(kernel, n), out_shape=(jax.ShapeDtypeStr...  108 us
    unnamed x10, local copies, waits for them, and re-layouts  4.23 us

profile of v2, /device:TPU:8, one launch (start us, length us, event | category | flops | bytes accessed | tf_op | source)
XLA Modules:
  0.0 114.6 jit_solution(15502230432280755744)
XLA Ops:
  0.6 0.7 broadcast_multiply_fusion
  1.3 0.1 iota_add_fusion
  1.4 0.7 add.26.codes
  2.0 108.3 %shard_map.111 = (bf16[128,1024]{1,0:T(8,128)(2,1)}, bf16[256,8192]{1,0:T(8,128)(2,1)S(1)}, f32[512,128]{1,0:T(8,128)}, f32[128,1024]{1,0:T(8,128)}) custom-call(s32[32]{0:T(128)} %plan.1, s32[32]{0:T(128)} %length.1, s32[32]{0:T(128)} %job.1, s32[1,512]{1,0:T(1,128)} %add.26.codes, bf16[256,8192]{1,0:T(8,128)(2,1)} %acts_in.1, bf16[128,1024]{1,0:T(8,128)(2,1)} %cot.1, ...), custom_call_target="tpu_custom_call" | custom-call | flops 8589934592 | bytes 8388608 | tf_op jit(solution)/shard_map/pallas_call | solution.py:529
  110.3 0.0 copy-start.2
  110.3 0.0 copy-start.1
  110.3 0.0 copy-start
  110.4 2.0 %copy.16 = bf16[256,8192]{1,0:T(8,128)(2,1)} copy(bf16[256,8192]{1,0:T(8,128)(2,1)S(1)} %get-tuple-element.5) | data formatting | bytes 8388608
  112.4 0.0 copy-done.2
  112.4 0.7 copy.17
  113.1 0.0 copy-done.1
  113.1 0.7 copy.18
  113.8 0.0 copy-done
  113.8 0.8 copy.19
Async XLA Ops:
  110.3 2.0 %copy-start.2 = (bf16[128,1024]{1,0:T(8,128)(2,1)S(1)}, bf16[128,1024]{1,0:T(8,128)(2,1)}, u32[]{:S(2)}) copy-start(bf16[128,1024]{1,0:T(8,128)(2,1)} %get-tuple-element.12) | copy-start | bytes 786436
  110.3 2.7 %copy-start.1 = (f32[512,128]{1,0:T(8,128)S(1)}, f32[512,128]{1,0:T(8,128)}, u32[]{:S(2)}) copy-start(f32[512,128]{1,0:T(8,128)} %get-tuple-element.14) | copy-start | bytes 786436
  110.3 3.4 %copy-start = (f32[128,1024]{1,0:T(8,128)S(1)}, f32[128,1024]{1,0:T(8,128)}, u32[]{:S(2)}) copy-start(f32[128,1024]{1,0:T(8,128)} %get-tuple-element.15) | copy-start | bytes 1572868
